TPU v7x, 256 devices: a whole 4x4x8 slice. The times are simulated.
256 devices in a mesh: row: 16 (over x, y), col: 16 (over z, core).
Axes of the slice: x: 4, y: 4, z: 8, core: 2. Of those that a mesh axis runs over, the one named last changes fastest.
Arguments:
- hidden_rows: bfloat16 [8192, 4096], P('row', 'col'), may hold values from -64 to 64
- code_table: bfloat16 [131072, 4096], P('row', 'col'), may hold values from -6 to 6
- labels: int32 [8192], P('row'), may hold values from 0 to 131071, as said below
- targets: int32 [8192], P('row'), may hold values from 0 to 8191
- sub_codebook: bfloat16 [4096, 8192], P('row', 'col'), may hold values from -1 to 1
Outputs:
- row_loss: float32 [8192], P('row')
- grad_hidden: bfloat16 [8192, 4096], P('row', 'col')
- grad_codes: bfloat16 [131072, 4096], P('row', 'col')
- grad_sub: bfloat16 [4096, 8192], P('row', 'col')
Inputs may be any that keep to these rules, and one draw needn't show every extreme that they name: Within each aligned block of 512 rows, at most 64 labels fall into any one aligned range of 8192 codes, and exactly 64 fall into some range.
All inputs are finite; a program needn't handle non-finite values.
Results may differ from a plain program's by a relative error of at most 0.022.
Values may be sent and summed in bfloat16 or wider, within the bound.
A program may use at most 128 MiB of HBM per device.

v0:
```python
import jax
import jax.numpy as jnp
from jax import lax
from jax.sharding import PartitionSpec as P


def per_device(hidden_rows, code_table, labels, targets, sub_codebook):
    row_count = labels.shape[0]
    groups = lax.axis_size("row")
    capacity = 2 * row_count // groups
    local_codes = code_table.shape[0]
    owner_group = labels // local_codes
    code_offset = labels % local_codes
    member_table = (owner_group[:, None] == jnp.arange(groups, dtype=jnp.int32)[None, :]).astype(
        jnp.int32
    )
    slot_rank = jnp.sum((jnp.cumsum(member_table, axis=0) - 1) * member_table, axis=1)
    slot_place = owner_group * capacity + slot_rank
    wanted = (
        jnp.zeros((groups * capacity,), jnp.int32)
        .at[slot_place]
        .set(code_offset)
        .reshape(groups, capacity)
    )
    asked_rows = lax.all_to_all(wanted, "row", split_axis=0, concat_axis=0, tiled=True)
    served = code_table[asked_rows.reshape(-1)].reshape(groups, capacity, code_table.shape[1])
    fetched = lax.all_to_all(served, "row", split_axis=0, concat_axis=0, tiled=True)
    code_part = fetched.reshape(groups * capacity, code_table.shape[1])[slot_place]
    query_part = (hidden_rows.astype(jnp.float32) + code_part.astype(jnp.float32)).astype(
        jnp.bfloat16
    )
    query_rows = lax.all_gather(query_part, "col", axis=1, tiled=True)
    full_weights = lax.all_gather(sub_codebook, "row", axis=0, tiled=True)
    logits = jnp.dot(query_rows, full_weights, preferred_element_type=jnp.float32)
    local_width = logits.shape[1]
    local_target = targets - lax.axis_index("col") * local_width
    target_hit = jnp.arange(local_width, dtype=jnp.int32)[None, :] == local_target[:, None]
    target_part = jnp.sum(jnp.where(target_hit, logits, 0.0), axis=1)
    local_peak = jnp.max(logits, axis=1)
    row_peak = lax.pmax(local_peak, "col")
    local_total = jnp.sum(jnp.exp(logits - row_peak[:, None]), axis=1)
    exp_total, target_logit = lax.psum((local_total, target_part), "col")
    log_total = row_peak + jnp.log(exp_total)
    row_loss = log_total - target_logit
    dlogits = (jnp.exp(logits - log_total[:, None]) - target_hit.astype(jnp.float32)).astype(
        jnp.bfloat16
    )
    partial_grad = lax.dot_general(
        dlogits, full_weights, (((1,), (1,)), ((), ())), preferred_element_type=jnp.float32
    )
    grad_query = lax.psum_scatter(
        partial_grad.astype(jnp.bfloat16), "col", scatter_dimension=1, tiled=True
    ).astype(jnp.float32)
    grad_hidden = grad_query.astype(jnp.bfloat16)
    outgoing = (
        jnp.zeros((groups * capacity, grad_query.shape[1]), jnp.float32)
        .at[slot_place]
        .set(grad_query)
    )
    returned = lax.all_to_all(
        outgoing.reshape(groups, capacity, grad_query.shape[1]).astype(jnp.bfloat16),
        "row",
        split_axis=0,
        concat_axis=0,
        tiled=True,
    ).astype(jnp.float32)
    grad_codes = (
        jnp.zeros((local_codes, code_table.shape[1]), jnp.float32)
        .at[asked_rows.reshape(-1)]
        .add(returned.reshape(groups * capacity, grad_query.shape[1]))
        .astype(jnp.bfloat16)
    )
    grad_sub = lax.psum_scatter(
        lax.dot_general(
            query_rows, dlogits, (((0,), (0,)), ((), ())), preferred_element_type=jnp.float32
        ).astype(jnp.bfloat16),
        "row",
        scatter_dimension=0,
        tiled=True,
    )
    return (row_loss, grad_hidden, grad_codes, grad_sub)


def solution(mesh):
    return jax.shard_map(
        per_device,
        mesh=mesh,
        in_specs=(P("row", "col"), P("row", "col"), P("row"), P("row"), P("row", "col")),
        out_specs=(P("row"), P("row", "col"), P("row", "col"), P("row", "col")),
        check_vma=False,
    )
```

profile of v0, /device:TPU:24, one launch (start us, length us, event | category | flops | bytes accessed | tf_op | source)
XLA Modules:
  0.0 336.1 jit_solution(9969947385769509341)
XLA Ops:
  7.2 0.7 all-gather.5.cloned.1.call-update
  7.9 0.7 add_select_fusion
  8.6 1.2 reduce-window.6
  10.1 2.4 scatter_custom_fusion
  12.7 12.5 %all_to_all.19 = s32[16,1,64]{2,1,0:T(1,128)S(1)} all-to-all(s32[16,1,64]{2,1,0:T(1,128)S(1)} %all_to_all.12), channel_id=1, replica_groups=mesh['row'=16,'col'=16] {'row'}, dimensions={0} | all-to-all | bytes 8192 | tf_op jit(solution)/shard_map/all_to_all | solution.py:25
  25.7 0.7 reduce.5
  26.5 7.3 %gather_fusion = bf16[1024,256]{1,0:T(8,128)(2,1)} fusion(bf16[8192,256]{1,0:T(8,128)(2,1)} %param.6, s32[1024]{0:T(1024)S(1)} %broadcast_clamp_fusion), kind=kCustom, calls=%fused_computation | custom fusion | bytes 1052672 | tf_op jit(solution)/shard_map/gather | solution.py:26
  33.9 5.4 %all-to-all-start.1 = ((bf16[16,64,256]{2,1,0:T(8,128)(2,1)}), bf16[16,64,256]{2,1,0:T(8,128)(2,1)S(1)}, u32[]{:S(2)}, u32[]{:S(2)}) async-start(bf16[16,64,256]{2,1,0:T(8,128)(2,1)} %bitcast.3), calls=%async_computation.1 | async-start | bytes 1048576 | tf_op jit(solution)/shard_map/all_to_all | solution.py:27
  39.4 7.7 %all-to-all-done.1 = bf16[16,64,256]{2,1,0:T(8,128)(2,1)S(1)} async-done(((bf16[16,64,256]{2,1,0:T(8,128)(2,1)}), bf16[16,64,256]{2,1,0:T(8,128)(2,1)S(1)}, u32[]{:S(2)}, u32[]{:S(2)}) %all-to-all-start.1) | async-done | bytes 524320 | tf_op jit(solution)/shard_map/all_to_all | solution.py:27
  47.1 1.9 gather_fusion.1
  49.1 0.8 add_convert_fusion
  49.9 19.7 %all-gather.5.cloned.1.call-done = bf16[4096,512]{1,0:T(8,128)(2,1)} async-done(((bf16[256,512]{1,0:T(8,128)(2,1)}), bf16[4096,512]{1,0:T(8,128)(2,1)}) %all-gather.5.cloned.1.call-update) | async-done | bytes 4194320 | tf_op jit(solution)/shard_map/all_gather | solution.py:33
  69.6 50.8 %all-gather.3.cloned.1.call-done = bf16[512,4096]{1,0:T(8,128)(2,1)} async-done(((bf16[512,256]{1,0:T(8,128)(2,1)}), bf16[512,4096]{1,0:T(8,128)(2,1)}) %all-gather.3.cloned.1.call-update) | async-done | bytes 4194320 | tf_op jit(solution)/shard_map/all_gather | solution.py:32
  120.4 5.9 %fusion.13 = (f32[512]{0:T(512)S(1)}, f32[512,512]{0,1:T(8,128)S(1)}) fusion(bf16[512,4096]{1,0:T(8,128)(2,1)} %all-gather.3.cloned.1.call-done, bf16[4096,512]{1,0:T(8,128)(2,1)} %all-gather.5.cloned.1.call-done), kind=kOutput, calls=%fused_computation.43 | convolution fusion | flops 2147745280 | bytes 9439232 | tf_op jit(solution)/shard_map/dot_general | solution.py:34
  126.3 26.3 %pmax.7 = f32[512]{0:T(512)S(1)} all-reduce(f32[512]{0:T(512)S(1)} %get-tuple-element.12), channel_id=1, replica_groups=mesh['row'=16,'col'=16] {'col'}, use_global_device_ids=true, to_apply=%region_5.6 | all-reduce | flops 512 | bytes 4096 | tf_op jit(solution)/shard_map/pmax | solution.py:40
  152.9 23.5 %all-reduce = (f32[512]{0:T(512)S(1)}, f32[512]{0:T(512)S(1)}) all-reduce(f32[512]{0:T(512)S(1)} %get-tuple-element.5, f32[512]{0:T(512)S(1)} %get-tuple-element.4), channel_id=1, replica_groups=mesh['row'=16,'col'=16] {'col'}, use_global_device_ids=true, to_apply=%region_7.8 | all-reduce | flops 1024 | bytes 8192 | tf_op jit(solution)/shard_map/psum | solution.py:42
  177.0 6.6 %convolution_convert_fusion.1 = bf16[512,4096]{1,0:T(8,128)(2,1)} fusion(bf16[4096,512]{1,0:T(8,128)(2,1)} %all-gather.5.cloned.1.call-done, f32[512,512]{0,1:T(8,128)S(1)} %get-tuple-element.13, f32[512]{0:T(512)S(1)} %get-tuple-element.9, s32[512]{0:T(512)S(1)} %broadcast_subtract_fusion), kind=kOutput, calls=%fused_computation.6 | convolution fusion | flops 2150891520 | bytes 9441280 | tf_op jit(solution)/shard_map/dot_general | solution.py:48
  183.9 6.6 %convolution_convert_fusion = bf16[4096,512]{1,0:T(8,128)(2,1)} fusion(bf16[512,4096]{1,0:T(8,128)(2,1)} %all-gather.3.cloned.1.call-done, f32[512,512]{0,1:T(8,128)S(1)} %get-tuple-element.13, f32[512]{0:T(512)S(1)} %get-tuple-element.9, s32[512]{0:T(512)S(1)} %broadcast_subtract_fusion), kind=kOutput, calls=%fused_computation.5 | convolution fusion | flops 2150891520 | bytes 9441280 | tf_op jit(solution)/shard_map/dot_general | solution.py:74
  190.6 54.0 %reduce-scatter.3.cloned.1.call-done = bf16[512,256]{1,0:T(8,128)(2,1)} async-done(((bf16[512,4096]{1,0:T(8,128)(2,1)}), bf16[512,256]{1,0:T(8,128)(2,1)}) %reduce-scatter.3.cloned.1.call-update) | async-done | bytes 262160 | tf_op jit(solution)/shard_map/reduce_scatter | solution.py:51
  244.6 2.9 scatter_custom_fusion.1
  247.6 14.5 %all_to_all.20 = bf16[16,64,256]{2,1,0:T(8,128)(2,1)S(1)} all-to-all(bf16[16,64,256]{2,1,0:T(8,128)(2,1)S(1)} %bitcast.30), channel_id=1, replica_groups=mesh['row'=16,'col'=16] {'row'}, dimensions={0} | all-to-all | bytes 1048576 | tf_op jit(solution)/shard_map/all_to_all | solution.py:60
  262.1 10.3 %scatter_custom_fusion.2 = f32[8192,256]{1,0:T(8,128)} fusion(s32[1024]{0:T(1024)S(1)} %bitcast.33, f32[]{:T(128)} %constant.51.clone.1, bf16[1024,256]{1,0:T(8,128)(2,1)S(1)} %bitcast.29), kind=kCustom, calls=%fused_computation.7 | custom fusion | flops 524288 | bytes 8912900 | tf_op jit(solution)/shard_map/scatter-add | solution.py:70
  272.5 5.9 %convert_element_type.50 = bf16[8192,256]{1,0:T(8,128)(2,1)} convert(f32[8192,256]{1,0:T(8,128)} %scatter_custom_fusion.2) | non-fusion elementwise | flops 2097152 | bytes 12582912 | tf_op jit(solution)/shard_map/convert_element_type | solution.py:71
  278.3 51.2 %reduce-scatter.5.cloned.1.call-done = bf16[256,512]{1,0:T(8,128)(2,1)} async-done(((bf16[4096,512]{1,0:T(8,128)(2,1)}), bf16[256,512]{1,0:T(8,128)(2,1)}) %reduce-scatter.5.cloned.1.call-update) | async-done | bytes 262160 | tf_op jit(solution)/shard_map/reduce_scatter | solution.py:73
  (27 shorter events, 2.4 us)
Async XLA Ops:
  7.2 62.5 %all-gather.5.cloned.1.call-start = ((), (), s32[]{:S(2)}) async-start(), calls=%async_computation.6 | async-start | bytes 4456448 | tf_op jit(solution)/shard_map/all_gather | solution.py:33
  8.6 40.4 %copy-start = (bf16[512,256]{1,0:T(8,128)(2,1)S(1)}, bf16[512,256]{1,0:T(8,128)(2,1)}, u32[]{:S(2)}) copy-start(bf16[512,256]{1,0:T(8,128)(2,1)} %param.5) | copy-start | bytes 786436
  26.5 23.4 %copy-start.1 = (s32[512]{0:T(512)S(1)}, s32[512]{0:T(512)}, u32[]{:S(2)}) copy-start(s32[512]{0:T(512)} %param.8) | copy-start | bytes 6148
  33.9 13.2 %all-to-all-start.1 = ((bf16[16,64,256]{2,1,0:T(8,128)(2,1)}), bf16[16,64,256]{2,1,0:T(8,128)(2,1)S(1)}, u32[]{:S(2)}, u32[]{:S(2)}) async-start(bf16[16,64,256]{2,1,0:T(8,128)(2,1)} %bitcast.3), calls=%async_computation.1 | async-start | bytes 1048576 | tf_op jit(solution)/shard_map/all_to_all | solution.py:27
  39.3 81.1 %all-gather.3.cloned.1.call-start = ((), (), s32[]{:S(2)}) async-start(), calls=%async_computation.5 | async-start | bytes 4456448 | tf_op jit(solution)/shard_map/all_gather | solution.py:32
  49.9 194.8 %reduce-scatter.3.cloned.1.call-start = ((), (), s32[]{:S(2)}) async-start(), calls=%async_computation.7 | async-start | bytes 4456448 | tf_op jit(solution)/shard_map/reduce_scatter | solution.py:51
  183.7 145.9 %reduce-scatter.5.cloned.1.call-start = ((), (), s32[]{:S(2)}) async-start(), calls=%async_computation.8 | async-start | bytes 4456448 | tf_op jit(solution)/shard_map/reduce_scatter | solution.py:73
Sparse Core Ops, SparseCore 0:
  10.4 59.1 all-gather.4
  72.0 48.3 all-gather.2
  183.8 60.7 reduce-scatter.2
  248.7 80.8 reduce-scatter.4
where the time goes:
time: 337 us; the launch traced here: 336 us
  waiting for transfers between devices  184 us (55%)
  blocking collectives  77 us (23%)
  other arithmetic  23.5 us (7%)
  matrix products  19.1 us (6%)
  between operations  13.9 us (4%)
  local copies, waits for them, and re-layouts  12.6 us (4%)
  starting transfers between devices  5.77 us (2%)
    reduce_scatter x1, waiting for transfers between devices, per_device(): lax.psum_scatter(partial_grad.astype(jnp.bfloat16), 'col', scatter_dimens...  54 us
    reduce_scatter x1, waiting for transfers between devices, per_device(): lax.psum_scatter(lax.dot_general(query_rows, dlogits, (((0,), (0,)), ((),...  51.2 us
    all_gather x1, waiting for transfers between devices, per_device(): query_rows = lax.all_gather(query_part, 'col', axis=1, tiled=True)  50.8 us
    pmax x1, blocking collectives, per_device(): row_peak = lax.pmax(local_peak, 'col')  26.3 us
    psum x1, blocking collectives, per_device(): exp_total, target_logit = lax.psum((local_total, target_part), 'col')  23.5 us
    all_gather x1, waiting for transfers between devices, per_device(): full_weights = lax.all_gather(sub_codebook, 'row', axis=0, tiled=True)  19.7 us
    all_to_all x1, blocking collectives, per_device(): lax.all_to_all(outgoing.reshape(groups, capacity, grad_query.shape[1]).as...  14.5 us
    all_to_all x1, blocking collectives, per_device(): lax.all_to_all(wanted, 'row', split_axis=0, concat_axis=0, tiled=True)  12.5 us
  transfers between devices with their start and end apart: 5, of which 5 were waited for; matrix products, arithmetic and copies ran while one was open for 12% of the time, Pallas kernels for 0%

commit v1 on v0

v1 whole, which is shorter than its diff:
```python
import jax
import jax.numpy as jnp
from jax import lax
from jax.experimental import pallas as pl
from jax.experimental.pallas import tpu as pltpu
from jax.sharding import PartitionSpec as P

MESH = pl.DeviceIdType.MESH
F32, BF16, I32 = jnp.float32, jnp.bfloat16, jnp.int32

NX, NY, NZ = 4, 4, 8
NR, NC = NX * NY, 2 * NZ
ROWS, FEAT, CODES = 512, 256, 512
HALF = 256
TABLE = 8192
CAP = 64
CHUNK = 1024
NT = (((1,), (1,)), ((), ()))


class Ids:
    def __init__(self):
        self.at = {}
        for name in ("want", "serve", "stat", "ret"):
            for rel in range(16):
                self((name, rel))
        for half in range(2):
            for j in range(5):
                for part in range(4):
                    self(("w", half, j, part))
                    self(("x", half, j, part))
        for way in (1, -1):
            for s in range(4):
                for h in range(2):
                    self(("q", way, s + 1, h))
                    self(("z", way, s, h))
        for dz in range(NZ):
            self(("gs", dz))
            for h in range(2):
                self(("qs", dz, h))

    def __call__(self, name):
        return self.at.setdefault(name, len(self.at))


IDS = Ids()
N_IDS = len(IDS.at)


def dot(a, b, dims=(((1,), (0,)), ((), ()))):
    return lax.dot_general(a, b, dims, preferred_element_type=F32)


def main_kernel(
    hid, table, lab, tgt, wsub,
    loss_o, gh_o, gs_o, ret_o, ask_o,
    wf, qf, tb, tf, wbuf, askv, asks, srv32, srv, fet, pm, mm, lg, dl, dlt,
    stat_s, stat_r, gqo, gqs, sibr, zr, gt, xq, xl, outb,
    lsem, ssem, rsem,
):
    row = lax.axis_index("row")
    col = lax.axis_index("col")
    x, y = row // NY, row % NY
    z, k = col // 2, col % 2

    def rdev(r):
        return (r, col)

    def cdev(c):
        return (row, c)

    def xn(d):
        return rdev(((x + d + NX) % NX) * NY + y)

    def yn(d):
        return rdev(x * NY + (y + d + NY) % NY)

    def zn(d):
        return cdev(((z + d + NZ) % NZ) * 2 + k)

    sib = cdev(z * 2 + 1 - k)

    def slot(dx, dy):
        return ((x + dx) % NX) * NY + (y + dy) % NY

    def cp(i, src, dst, dev):
        return pltpu.make_async_remote_copy(
            src_ref=src, dst_ref=dst, send_sem=ssem.at[i], recv_sem=rsem.at[i],
            device_id=dev, device_id_type=MESH,
        )

    sent = []

    def send(name, src, dst, dev):
        c = cp(IDS(name), src, dst, dev)
        c.start()
        sent.append(c)

    def recv(name, dst):
        cp(IDS(name), dst, dst, sib).wait_recv()

    own_w = pltpu.make_async_copy(wsub, wf.at[row], lsem.at[0])
    own_w.start()

    def table_copy(i):
        return pltpu.make_async_copy(
            table.at[pl.ds(i * CHUNK, CHUNK), :], tb.at[i % 2], lsem.at[2 + i % 2]
        )

    table_copy(0).start()
    table_copy(1).start()

    barrier = pltpu.get_barrier_semaphore()
    for rel in range(1, 16):
        pl.semaphore_signal(barrier, inc=1, device_id=rdev((row + rel) % NR), device_id_type=MESH)
        pl.semaphore_signal(barrier, inc=1, device_id=cdev((col + rel) % NC), device_id_type=MESH)

    lab_row = jnp.concatenate([lab[i:i + 1, :] for i in range(4)], axis=1)
    owner = lax.shift_right_logical(lab_row, 13)
    off = lab_row & (TABLE - 1)
    member = (owner == lax.broadcasted_iota(I32, (NR, ROWS), 0)).astype(F32)
    before = (
        lax.broadcasted_iota(I32, (ROWS, ROWS), 0) < lax.broadcasted_iota(I32, (ROWS, ROWS), 1)
    ).astype(F32).astype(BF16)
    rank = jnp.sum(member * dot(member.astype(BF16), before), axis=0, keepdims=True)
    rank = rank.astype(I32)
    at_rank = (rank == lax.broadcasted_iota(I32, (128, ROWS), 0)).astype(F32).astype(BF16)
    hi = lax.shift_right_logical(off, 7).astype(F32)
    lo = (off & 127).astype(F32)
    both = jnp.concatenate([member * hi, member * lo], axis=0).astype(BF16)
    spread = dot(both, at_rank, NT)
    wanted = (spread[:NR] * 128.0 + spread[NR:]).astype(I32)
    for g in range(NR):
        wbuf[g] = jnp.broadcast_to(wanted[g:g + 1, :], (8, 128))
    place = owner * CAP + rank

    pl.semaphore_wait(barrier, 30)
    for rel in range(1, NR):
        to = (row + rel) % NR
        send(("want", rel), wbuf.at[to], askv.at[row], rdev(to))
    own_w.wait()

    def whalf(s, half, a=0, n=128):
        return wf.at[s, pl.ds(half * 128 + a, n), :]

    def wring(half, j):
        if j == 4:
            return (xn, lambda d: slot(d, 0)) if half == 0 else (yn, lambda d: slot(0, d))
        if half == 0:
            return yn, lambda d: slot(j, d)
        return xn, lambda d: slot(d, j)

    def w_own(half, j):
        nb, at = wring(half, j)
        send(("w", half, j, 0), whalf(at(0), half), whalf(at(0), half), nb(1))
        send(("w", half, j, 1), whalf(at(0), half), whalf(at(0), half), nb(-1))

    def w_mid(half, j, side):
        nb, at = wring(half, j)
        s = at(3) if side == 0 else at(1)
        recv(("w", half, j, side), whalf(s, half))
        part = whalf(s, half, 64 * side, 64)
        send(("w", half, j, 2 + side), part, part, nb(1 - 2 * side))

    def w_last(half, j):
        nb, at = wring(half, j)
        for side in range(2):
            recv(("w", half, j, 2 + side), whalf(at(2), half, 64 * side, 64))

    for half in range(2):
        w_own(half, 4)
    for half in range(2):
        w_own(half, 0)

    for i in range(TABLE // CHUNK):
        table_copy(i).wait()

        @pl.loop(0, CHUNK // 128)
        def _(t, i=i):
            tf[pl.ds(i * CHUNK + t * 128, 128), :] = tb[i % 2, pl.ds(t * 128, 128), :].astype(F32)

        if i + 2 < TABLE // CHUNK:
            table_copy(i + 2).start()

    askv[row] = wbuf[row]
    for rel in range(1, NR):
        recv(("want", rel), askv.at[(row - rel + NR) % NR])
    for r in range(NR):
        ask_o[r:r + 1, :] = askv[r, 0:1, :]
    to_smem = pltpu.make_async_copy(ask_o, asks, lsem.at[1])
    to_smem.start()
    to_smem.wait()

    def gather(r):
        @pl.loop(0, CAP // 8)
        def _(t):
            for u in range(8):
                i = asks[r, t * 8 + u] & (TABLE - 1)
                srv32[pl.ds(t * 8 + u, 1), :] = tf[pl.ds(i, 1), :]

    @pl.loop(1, NR)
    def _(rel):
        to = (row + rel) % NR
        gather(to)
        srv[to] = srv32[...].astype(BF16)
        cp(IDS(("serve", 0)) + rel, srv.at[to], fet.at[row], rdev(to)).start()

    gather(row)
    fet[row] = srv32[...].astype(BF16)

    place_f = place.astype(F32)
    for i in range(4):
        wide = jnp.broadcast_to(place_f[:, i * 128:(i + 1) * 128], (128, 128)).T.astype(I32)
        for t in range(8):
            pm[i * 128:(i + 1) * 128, t * 128:(t + 1) * 128] = (
                wide == lax.broadcasted_iota(I32, (128, 128), 1) + t * 128
            ).astype(F32).astype(BF16)
    for t in range(8):
        mm[t * 128:(t + 1) * 128, :] = (
            place == lax.broadcasted_iota(I32, (128, ROWS), 0) + t * 128
        ).astype(F32).astype(BF16)

    for half in range(2):
        for side in range(2):
            w_mid(half, 4, side)
            w_own(half, 3 - 2 * side)

    for rel in range(1, NR):
        recv(("serve", rel), fet.at[(row - rel + NR) % NR])

    def qpart(s, h):
        return qf.at[s, pl.ds(h * HALF, HALF), :]

    for h in range(2):
        rows = pl.ds(h * HALF, HALF)
        code = dot(pm[rows, :], fet[...].reshape(NR * CAP, FEAT))
        qf[col, rows, :] = (hid[rows, :].astype(F32) + code).astype(BF16)
        for way in (1, -1):
            send(("q", way, 1, h), qpart(col, h), qpart(col, h), zn(way))
        send(("qs", 0, h), qpart(col, h), qpart(col, h), sib)

    def q_step(s):
        for h in range(2):
            for way in (1, -1):
                if s == 4 and (way == 1) != (h == 0):
                    continue
                at = ((z - way * s + NZ) % NZ) * 2 + k
                piece = qpart(at, h)
                recv(("q", way, s, h), piece)
                if s < 3 or (s == 3 and (way == 1) == (h == 0)):
                    send(("q", way, s + 1, h), piece, piece, zn(way))
                send(("qs", (-way * s) % NZ, h), piece, piece, sib)

    def logits_of(n_ways, s):
        for dz in ([s, NZ - s] if 0 < s < 4 else [s]):
            for h in range(2):
                recv(("qs", dz, h), qpart(((z + dz) % NZ) * 2 + 1 - k, h))

        @pl.loop(0, 2 * n_ways)
        def _(t):
            dz = jnp.where(t % n_ways == 0, s, NZ - s)
            core = t // n_ways
            at = ((z + dz) % NZ) * 2 + core
            for h in range(2):
                rows = pl.ds(h * HALF, HALF)
                lg[rows, :] += dot(qf[at, rows, :], wf[at])

    for half in range(2):
        for side in range(2):
            w_mid(half, 0, side)
    for half in range(2):
        w_last(half, 4)
        w_own(half, 2)
    q_step(1)
    for j in (3, 1):
        for half in range(2):
            for side in range(2):
                w_mid(half, j, side)
    q_step(2)
    for half in range(2):
        for side in range(2):
            w_mid(half, 2, side)
    for j in (0, 3, 1, 2):
        for half in range(2):
            w_last(half, j)
    lg[...] = jnp.zeros((ROWS, CODES), F32)
    logits_of(1, 0)
    q_step(3)
    logits_of(2, 1)
    logits_of(2, 2)
    q_step(4)
    logits_of(2, 3)
    logits_of(1, 4)

    lane = lax.broadcasted_iota(I32, (128, 128), 1)

    def hit_of(i, j):
        wide = jnp.broadcast_to(tgt[i:i + 1, :].astype(F32), (128, 128)).T.astype(I32)
        return wide - col * CODES == lane + j * 128

    for i in range(4):
        rows = slice(i * 128, (i + 1) * 128)
        v = lg[rows, :]
        peak = jnp.max(v, axis=1, keepdims=True)
        log_sum = peak + jnp.log(jnp.sum(jnp.exp(v - peak), axis=1, keepdims=True))
        hits = jnp.concatenate([hit_of(i, j) for j in range(4)], axis=1)
        target = jnp.sum(jnp.where(hits, v, 0.0), axis=1, keepdims=True)
        pair = jnp.where(lane == 0, log_sum, jnp.where(lane == 1, target, 0.0)).T
        stat_s[i:i + 1, :] = pair[0:1, :]
        stat_s[4 + i:5 + i, :] = pair[1:2, :]
    stat_r[col] = stat_s[...]
    for rel in range(1, NC):
        send(("stat", rel), stat_s, stat_r.at[col], cdev((col + rel) % NC))
    for rel in range(1, NC):
        recv(("stat", rel), stat_r.at[(col - rel + NC) % NC])
    logs = stat_r[:, 0:4, :]
    top = jnp.max(logs, axis=0)
    log_total = top + jnp.log(jnp.sum(jnp.exp(logs - top[None]), axis=0))
    loss_o[...] = log_total - jnp.sum(stat_r[:, 4:8, :], axis=0)
    for i in range(4):
        wide = jnp.broadcast_to(log_total[i:i + 1, :], (128, 128)).T
        for j in range(4):
            v = lg[i * 128:(i + 1) * 128, j * 128:(j + 1) * 128]
            d = jnp.exp(v - wide) - hit_of(i, j).astype(F32)
            dl[i * 128:(i + 1) * 128, j * 128:(j + 1) * 128] = d.astype(BF16)
            dlt[j * 128:(j + 1) * 128, i * 128:(i + 1) * 128] = d.T.astype(BF16)

    def grad_block(dz):
        at = ((z + dz) % NZ) * 2
        gqs[dz] = dot(dl[...], wf[at + 1 - k], NT).astype(BF16)
        send(("gs", dz), gqs.at[dz], sibr.at[dz], sib)
        gqo[dz] = dot(dl[...], wf[at + k], NT).astype(BF16)

    def pair_up(dz):
        recv(("gs", dz), sibr.at[dz])
        gqo[dz] = (gqo[dz].astype(F32) + sibr[dz].astype(F32)).astype(BF16)

    def sub_block(dx, dy):
        s = slot(dx, dy)
        gt[s] = dot(dlt[...], qf[s]).astype(BF16)

    def zpart(dz, h):
        return gqo.at[dz % NZ, pl.ds(h * HALF, HALF), :]

    def zsend(way, d, h):
        send(("z", way, d, h), zpart(way * (d + 1), h), zr.at[(1 - way) // 2, d, h], zn(way))

    def zadd(way, d, h):
        got = zr.at[(1 - way) // 2, d, h]
        recv(("z", way, d, h), got)
        part = zpart(way * d, h)
        part[...] = (part[...].astype(F32) + got[...].astype(F32)).astype(BF16)

    def xring(half, j):
        if j == 4:
            return (xn, lambda d: slot(d, 0)) if half == 0 else (yn, lambda d: slot(0, d))
        if half == 0:
            return yn, lambda d: slot(j, d)
        return xn, lambda d: slot(d, j)

    def xpart(s, half, a=0, n=256):
        return gt.at[s, pl.ds(half * 256 + a, n), :]

    def x_start(half, j):
        nb, at = xring(half, j)
        for side in range(2):
            send(("x", half, j, side), xpart(at(2), half, 128 * side, 128), xq.at[half, j, side], nb(1 - 2 * side))

    def x_mid(half, j):
        nb, at = xring(half, j)
        for side in range(2):
            got = xq.at[half, j, side]
            recv(("x", half, j, side), got)
            s = at(1) if side == 0 else at(3)
            part = xpart(s, half, 128 * side, 128)
            part[...] = (part[...].astype(F32) + got[...].astype(F32)).astype(BF16)
            send(("x", half, j, 2 + side), xpart(s, half), xl.at[half, j, side], nb(1 - 2 * side))

    def x_end(half, j):
        nb, at = xring(half, j)
        for side in range(2):
            recv(("x", half, j, 2 + side), xl.at[half, j, side])
        part = xpart(at(0), half)
        part[...] = (
            part[...].astype(F32) + xl[half, j, 0].astype(F32) + xl[half, j, 1].astype(F32)
        ).astype(BF16)

    grad_block(4)
    grad_block(3)
    grad_block(5)
    sub_block(2, 2)
    pair_up(4)
    zsend(1, 3, 0)
    zsend(-1, 3, 1)
    for half in range(2):
        x_start(half, 2)
    pair_up(3)
    pair_up(5)
    zsend(1, 2, 1)
    zsend(-1, 2, 0)
    for d in (1, 3, 0):
        sub_block(2, d)
        sub_block(d, 2)
        for half in range(2):
            x_start(half, d)
    grad_block(2)
    grad_block(6)
    for half in range(2):
        x_mid(half, 2)
    pair_up(2)
    pair_up(6)
    for way, h in ((1, 0), (-1, 1)):
        zadd(way, 3, h)
        zsend(way, 2, h)
    sub_block(1, 1)
    sub_block(3, 1)
    sub_block(1, 3)
    sub_block(3, 3)
    sub_block(1, 0)
    sub_block(0, 1)
    sub_block(3, 0)
    sub_block(0, 3)
    sub_block(0, 0)
    for j in (1, 3):
        for half in range(2):
            x_mid(half, j)
    for way, h in ((1, 1), (-1, 0)):
        zadd(way, 2, h)
        zsend(way, 1, h)
    grad_block(1)
    grad_block(7)
    grad_block(0)
    for half in range(2):
        x_end(half, 2)
        x_start(half, 4)
    for half in range(2):
        x_mid(half, 0)
    pair_up(1)
    pair_up(7)
    for way, h in ((1, 0), (-1, 1)):
        zadd(way, 2, h)
        zsend(way, 1, h)
    for way, h in ((1, 1), (-1, 0)):
        zadd(way, 1, h)
        zsend(way, 0, h)
    for half in range(2):
        x_end(half, 1)
        x_end(half, 3)
    for half in range(2):
        x_mid(half, 4)
    for way, h in ((1, 0), (-1, 1)):
        zadd(way, 1, h)
        zsend(way, 0, h)
    pair_up(0)
    for half in range(2):
        x_end(half, 0)

    for way in (1, -1):
        for h in range(2):
            recv(("z", way, 0, h), zr.at[(1 - way) // 2, 0, h])
    for h in range(2):
        rows = pl.ds(h * HALF, HALF)
        total = gqo[0, rows, :].astype(F32) + zr[0, 0, h].astype(F32) + zr[1, 0, h].astype(F32)
        gh_o[rows, :] = total.astype(BF16)
    for t in range(8):
        moved = dot(mm[t * 128:(t + 1) * 128, :], gh_o[...]).astype(BF16)
        outb[2 * t] = moved[:CAP]
        outb[2 * t + 1] = moved[CAP:]
    for rel in range(1, NR):
        to = (row + rel) % NR
        send(("ret", rel), outb.at[to], ret_o.at[row], rdev(to))
    ret_o[row] = outb[row]
    for half in range(2):
        x_end(half, 4)
    gs_o[...] = gt[row].astype(F32).T.astype(BF16)
    for rel in range(1, NR):
        recv(("ret", rel), ret_o.at[(row - rel + NR) % NR])

    for c in sent:
        c.wait_send()

    @pl.loop(1, NR)
    def _(rel):
        cp(IDS(("serve", 0)) + rel, srv.at[0], fet.at[0], sib).wait_send()


def scatter_kernel(ret, ask, out):
    base = pl.program_id(0) * 256
    hits = (ask[...] - base == lax.broadcasted_iota(I32, (256, NR * CAP), 0)).astype(F32).astype(BF16)
    out[...] = dot(hits, ret[...]).astype(BF16)


def per_device(hidden_rows, code_table, labels, targets, sub_codebook):
    vmem = pl.BlockSpec(memory_space=pltpu.VMEM)
    loss, grad_hidden, grad_sub, returned, asked = pl.pallas_call(
        main_kernel,
        out_shape=(
            jax.ShapeDtypeStruct((4, 128), F32),
            jax.ShapeDtypeStruct((ROWS, FEAT), BF16),
            jax.ShapeDtypeStruct((FEAT, CODES), BF16),
            jax.ShapeDtypeStruct((NR, CAP, FEAT), BF16),
            jax.ShapeDtypeStruct((NR, 128), I32),
        ),
        in_specs=[vmem, pl.BlockSpec(memory_space=pl.ANY), vmem, vmem, vmem],
        out_specs=[vmem] * 5,
        scratch_shapes=[
            pltpu.VMEM((NR, FEAT, CODES), BF16),
            pltpu.VMEM((NC, ROWS, FEAT), BF16),
            pltpu.VMEM((2, CHUNK, FEAT), BF16),
            pltpu.VMEM((TABLE, FEAT), F32),
            pltpu.VMEM((NR, 8, 128), I32),
            pltpu.VMEM((NR, 8, 128), I32),
            pltpu.SMEM((NR, 128), I32),
            pltpu.VMEM((CAP, FEAT), F32),
            pltpu.VMEM((NR, CAP, FEAT), BF16),
            pltpu.VMEM((NR, CAP, FEAT), BF16),
            pltpu.VMEM((ROWS, NR * CAP), BF16),
            pltpu.VMEM((NR * CAP, ROWS), BF16),
            pltpu.VMEM((ROWS, CODES), F32),
            pltpu.VMEM((ROWS, CODES), BF16),
            pltpu.VMEM((CODES, ROWS), BF16),
            pltpu.VMEM((8, 128), F32),
            pltpu.VMEM((NC, 8, 128), F32),
            pltpu.VMEM((NZ, ROWS, FEAT), BF16),
            pltpu.VMEM((NZ, ROWS, FEAT), BF16),
            pltpu.VMEM((NZ, ROWS, FEAT), BF16),
            pltpu.VMEM((2, 4, 2, HALF, FEAT), BF16),
            pltpu.VMEM((NR, CODES, FEAT), BF16),
            pltpu.VMEM((2, 5, 2, 128, FEAT), BF16),
            pltpu.VMEM((2, 5, 2, 256, FEAT), BF16),
            pltpu.VMEM((NR, CAP, FEAT), BF16),
            pltpu.SemaphoreType.DMA((4,)),
            pltpu.SemaphoreType.DMA((N_IDS,)),
            pltpu.SemaphoreType.DMA((N_IDS,)),
        ],
        compiler_params=pltpu.CompilerParams(
            collective_id=0, has_side_effects=True, vmem_limit_bytes=60 * 1024 * 1024
        ),
        name="exchange_and_gradients",
    )(hidden_rows, code_table, labels.reshape(4, 128), targets.reshape(4, 128), sub_codebook)
    grad_codes = pl.pallas_call(
        scatter_kernel,
        grid=(TABLE // 256,),
        in_specs=[
            pl.BlockSpec((NR * CAP, FEAT), lambda i: (0, 0)),
            pl.BlockSpec((1, NR * CAP), lambda i: (0, 0)),
        ],
        out_specs=pl.BlockSpec((256, FEAT), lambda i: (i, 0)),
        out_shape=jax.ShapeDtypeStruct((TABLE, FEAT), BF16),
        name="grad_codes",
    )(returned.reshape(NR * CAP, FEAT), asked[:, :CAP].reshape(1, NR * CAP))
    return loss.reshape(ROWS), grad_hidden, grad_codes, grad_sub


def solution(mesh):
    return jax.shard_map(
        per_device,
        mesh=mesh,
        in_specs=(P("row", "col"), P("row", "col"), P("row"), P("row"), P("row", "col")),
        out_specs=(P("row"), P("row", "col"), P("row", "col"), P("row", "col")),
        check_vma=False,
    )
```

time: 337 us -> 120 us (0.36)
  waiting for transfers between devices: 184 us -> 0 us
  Pallas kernels: 0 us -> 116 us
  blocking collectives: 77 us -> 0 us
  other arithmetic: 23.5 us -> 0 us
  matrix products: 19.1 us -> 0 us
  between operations: 13.9 us -> 0.67 us
  local copies, waits for them, and re-layouts: 12.6 us -> 3.42 us
  starting transfers between devices: 5.77 us -> 0 us
    pallas_call x0 -> x2, Pallas kernels: none -> 116 us  [the longest x1 98.6 us: per_device(): pl.pallas_call(main_kernel, out_shape=(jax.ShapeDtypeStruct((4, 128), F32...]
    reduce_scatter x2 -> x0, waiting for transfers between devices: 105 us -> none  [the longest x1 54 us: per_device(): lax.psum_scatter(partial_grad.astype(jnp.bfloat16), 'col', scatter_dimens...]
    all_gather x2 -> x0, waiting for transfers between devices: 70.5 us -> none  [the longest x1 50.8 us: per_device(): query_rows = lax.all_gather(query_part, 'col', axis=1, tiled=True)]
    all_to_all x2 -> x0, blocking collectives: 27.1 us -> none  [the longest x1 14.5 us: per_device(): lax.all_to_all(outgoing.reshape(groups, capacity, grad_query.shape[1]).as...]
    pmax x1 -> x0, blocking collectives: 26.3 us -> none  [per_device(): row_peak = lax.pmax(local_peak, 'col')]
    psum x1 -> x0, blocking collectives: 23.5 us -> none  [per_device(): exp_total, target_logit = lax.psum((local_total, target_part), 'col')]
    dot_general x3 -> x0, matrix products: 19.1 us -> none  [the longest x1 6.64 us: per_device(): lax.dot_general(dlogits, full_weights, (((1,), (1,)), ((), ())), preferre...]
    scatter-add x1 -> x0, other arithmetic: 10.3 us -> none  [per_device(): grad_codes = jnp.zeros((local_codes, code_table.shape[1]), jnp.float32).a...]
  transfers between devices with their start and end apart: 5 -> 0, of which waited for: 5 -> 0; matrix products, arithmetic and copies ran while one was open for 12% -> 0% of each run, Pallas kernels for 0% -> 0%
where the time goes in v1:
time: 120 us
  Pallas kernels  116 us (97%)
  local copies, waits for them, and re-layouts  3.42 us (3%)
    pallas_call x1, Pallas kernels, per_device(): pl.pallas_call(main_kernel, out_shape=(jax.ShapeDtypeStruct((4, 128), F32...  98.6 us
    pallas_call x1, Pallas kernels, per_device(): pl.pallas_call(scatter_kernel, grid=(TABLE // 256,), in_specs=[pl.BlockSp...  17 us

profile of v1, /device:TPU:24, one launch (start us, length us, event | category | flops | bytes accessed | tf_op | source)
XLA Modules:
  0.0 119.7 jit_solution(5795428829897445105)
XLA Ops:
  0.6 98.6 %exchange_and_gradients.1 = (f32[4,128]{1,0:T(4,128)}, bf16[512,256]{1,0:T(8,128)(2,1)}, bf16[256,512]{1,0:T(8,128)(2,1)}, bf16[16,64,256]{2,1,0:T(8,128)(2,1)}, s32[16,128]{1,0:T(8,128)}) custom-call(bf16[512,256]{1,0:T(8,128)(2,1)} %hid.1, bf16[8192,256]{1,0:T(8,128)(2,1)} %table.1, s32[4,128]{1,0:T(4,128)} %bitcast.7, s32[4,128]{1,0:T(4,128)} %bitcast.8, ...), custom_call_target="tpu_custom_call" | custom-call | tf_op jit(solution)/shard_map/exchange_and_gradients/pallas_call | solution.py:495
  99.2 0.0 copy-start.2
  99.2 0.0 copy-start.1
  99.2 0.0 copy-start
  99.3 1.4 %reshape.27.ask = s32[1,1024]{1,0:T(1,128)} reshape(s32[16,64]{1,0:T(8,128)} %bitcast.6) | data formatting | bytes 8192 | tf_op jit(solution)/shard_map/reshape | solution.py:551
  100.7 17.0 %grad_codes.1 = bf16[8192,256]{1,0:T(8,128)(2,1)} custom-call(bf16[1024,256]{1,0:T(8,128)(2,1)} %bitcast.5, s32[1,1024]{1,0:T(1,128)} %reshape.27.ask), custom_call_target="tpu_custom_call" | custom-call | tf_op jit(solution)/shard_map/grad_codes/pallas_call | solution.py:541
  117.7 0.0 copy-done.2
  117.7 0.6 copy.12
  118.3 0.0 copy-done.1
  118.3 0.7 copy.13
  119.0 0.0 copy-done
  119.0 0.7 copy.14
Async XLA Ops:
  99.2 18.5 %copy-start.2 = (f32[4,128]{1,0:T(4,128)S(1)}, f32[4,128]{1,0:T(4,128)}, u32[]{:S(2)}) copy-start(f32[4,128]{1,0:T(4,128)} %get-tuple-element.9) | copy-start | bytes 6148
  99.2 19.0 %copy-start.1 = (bf16[512,256]{1,0:T(8,128)(2,1)S(1)}, bf16[512,256]{1,0:T(8,128)(2,1)}, u32[]{:S(2)}) copy-start(bf16[512,256]{1,0:T(8,128)(2,1)} %get-tuple-element.19) | copy-start | bytes 786436
  99.2 19.7 %copy-start = (bf16[256,512]{1,0:T(8,128)(2,1)S(1)}, bf16[256,512]{1,0:T(8,128)(2,1)}, u32[]{:S(2)}) copy-start(bf16[256,512]{1,0:T(8,128)(2,1)} %get-tuple-element.21) | copy-start | bytes 786436

commit v2 on v1

--- a/solution.py
+++ b/solution.py
@@ -15,13 +15,14 @@
 TABLE = 8192
 CAP = 64
 CHUNK = 1024
+TILE = 2048
 NT = (((1,), (1,)), ((), ()))
 
 
 class Ids:
     def __init__(self):
         self.at = {}
-        for name in ("want", "serve", "stat", "ret"):
+        for name in ("want", "serve0", "serve1", "stat", "ret0", "ret1"):
             for rel in range(16):
                 self((name, rel))
         for half in range(2):
@@ -54,9 +55,9 @@
 def main_kernel(
     hid, table, lab, tgt, wsub,
     loss_o, gh_o, gs_o, ret_o, ask_o,
-    wf, qf, tb, tf, wbuf, askv, asks, srv32, srv, fet, pm, mm, lg, dl, dlt,
-    stat_s, stat_r, gqo, gqs, sibr, zr, gt, xq, xl, outb,
-    lsem, ssem, rsem,
+    wf, qf, tb, tf, wbuf, askv, askr, asks, srv32, srv, fet, pm, mm, tw, lg, dl, dlt,
+    stat_s, stat_r, gqo, gqs, sibr, zr, gt, xq, xl, ghb, outb,
+    lsem, tsem, ssem, rsem,
 ):
     row = lax.axis_index("row")
     col = lax.axis_index("col")
@@ -104,11 +105,11 @@
 
     def table_copy(i):
         return pltpu.make_async_copy(
-            table.at[pl.ds(i * CHUNK, CHUNK), :], tb.at[i % 2], lsem.at[2 + i % 2]
+            table.at[pl.ds(i * CHUNK, CHUNK), :], tb.at[i], tsem.at[i]
         )
 
-    table_copy(0).start()
-    table_copy(1).start()
+    for i in range(TABLE // CHUNK):
+        table_copy(i).start()
 
     barrier = pltpu.get_barrier_semaphore()
     for rel in range(1, 16):
@@ -177,64 +178,62 @@
 
         @pl.loop(0, CHUNK // 128)
         def _(t, i=i):
-            tf[pl.ds(i * CHUNK + t * 128, 128), :] = tb[i % 2, pl.ds(t * 128, 128), :].astype(F32)
-
-        if i + 2 < TABLE // CHUNK:
-            table_copy(i + 2).start()
+            v = tb[i, pl.ds(t * 128, 128), :].astype(F32)
+            for h in range(2):
+                tf[h, pl.ds(i * CHUNK + t * 128, 128), :] = v[:, h * 128:(h + 1) * 128]
+
+    place_f = place.astype(F32)
+    lane = lax.broadcasted_iota(I32, (128, 128), 1)
+    for i in range(4):
+        wide = jnp.broadcast_to(place_f[:, i * 128:(i + 1) * 128], (128, 128)).T.astype(I32)
+        for t in range(8):
+            pm[i * 128:(i + 1) * 128, t * 128:(t + 1) * 128] = (
+                wide == lane + t * 128
+            ).astype(F32).astype(BF16)
 
     askv[row] = wbuf[row]
     for rel in range(1, NR):
         recv(("want", rel), askv.at[(row - rel + NR) % NR])
     for r in range(NR):
-        ask_o[r:r + 1, :] = askv[r, 0:1, :]
-    to_smem = pltpu.make_async_copy(ask_o, asks, lsem.at[1])
+        askr[r:r + 1, :] = askv[r, 0:1, :]
+    to_smem = pltpu.make_async_copy(askr, asks, lsem.at[1])
     to_smem.start()
     to_smem.wait()
 
-    def gather(r):
-        @pl.loop(0, CAP // 8)
+    def gather(h, r):
+        @pl.loop(0, CAP // 16)
         def _(t):
-            for u in range(8):
-                i = asks[r, t * 8 + u] & (TABLE - 1)
-                srv32[pl.ds(t * 8 + u, 1), :] = tf[pl.ds(i, 1), :]
-
-    @pl.loop(1, NR)
-    def _(rel):
-        to = (row + rel) % NR
-        gather(to)
-        srv[to] = srv32[...].astype(BF16)
-        cp(IDS(("serve", 0)) + rel, srv.at[to], fet.at[row], rdev(to)).start()
-
-    gather(row)
-    fet[row] = srv32[...].astype(BF16)
-
-    place_f = place.astype(F32)
-    for i in range(4):
-        wide = jnp.broadcast_to(place_f[:, i * 128:(i + 1) * 128], (128, 128)).T.astype(I32)
-        for t in range(8):
-            pm[i * 128:(i + 1) * 128, t * 128:(t + 1) * 128] = (
-                wide == lax.broadcasted_iota(I32, (128, 128), 1) + t * 128
-            ).astype(F32).astype(BF16)
-    for t in range(8):
-        mm[t * 128:(t + 1) * 128, :] = (
-            place == lax.broadcasted_iota(I32, (128, ROWS), 0) + t * 128
-        ).astype(F32).astype(BF16)
+            for u in range(16):
+                i = asks[r, t * 16 + u] & (TABLE - 1)
+                srv32[pl.ds(t * 16 + u, 1), :] = tf[h, pl.ds(i, 1), :]
+
+    for h in range(2):
+        @pl.loop(1, NR)
+        def _(rel, h=h):
+            to = (row + rel) % NR
+            gather(h, to)
+            srv[h, to] = srv32[...].astype(BF16)
+            cp(IDS((f"serve{h}", 0)) + rel, srv.at[h, to], fet.at[h, row], rdev(to)).start()
+
+        gather(h, row)
+        fet[h, row] = srv32[...].astype(BF16)
 
     for half in range(2):
         for side in range(2):
             w_mid(half, 4, side)
             w_own(half, 3 - 2 * side)
-
-    for rel in range(1, NR):
-        recv(("serve", rel), fet.at[(row - rel + NR) % NR])
+    for half in range(2):
+        for side in range(2):
+            w_mid(half, 0, side)
 
     def qpart(s, h):
-        return qf.at[s, pl.ds(h * HALF, HALF), :]
+        return qf.at[s, h]
 
     for h in range(2):
-        rows = pl.ds(h * HALF, HALF)
-        code = dot(pm[rows, :], fet[...].reshape(NR * CAP, FEAT))
-        qf[col, rows, :] = (hid[rows, :].astype(F32) + code).astype(BF16)
+        for rel in range(1, NR):
+            recv((f"serve{h}", rel), fet.at[h, (row - rel + NR) % NR])
+        code = dot(pm[...], fet[h].reshape(NR * CAP, 128))
+        qf[col, h] = (hid[:, h * 128:(h + 1) * 128].astype(F32) + code).astype(BF16)
         for way in (1, -1):
             send(("q", way, 1, h), qpart(col, h), qpart(col, h), zn(way))
         send(("qs", 0, h), qpart(col, h), qpart(col, h), sib)
@@ -263,14 +262,20 @@
             at = ((z + dz) % NZ) * 2 + core
             for h in range(2):
                 rows = pl.ds(h * HALF, HALF)
-                lg[rows, :] += dot(qf[at, rows, :], wf[at])
-
-    for half in range(2):
-        for side in range(2):
-            w_mid(half, 0, side)
+                q = jnp.concatenate([qf[at, 0, rows, :], qf[at, 1, rows, :]], axis=1)
+                lg[rows, :] += dot(q, wf[at])
+
     for half in range(2):
         w_last(half, 4)
         w_own(half, 2)
+    for i in range(4):
+        tw[i * 128:(i + 1) * 128, :] = (
+            jnp.broadcast_to(tgt[i:i + 1, :].astype(F32), (128, 128)).T.astype(I32) - col * CODES
+        )
+    for t in range(8):
+        mm[t * 128:(t + 1) * 128, :] = (
+            place == lax.broadcasted_iota(I32, (128, ROWS), 0) + t * 128
+        ).astype(F32).astype(BF16)
     q_step(1)
     for j in (3, 1):
         for half in range(2):
@@ -292,11 +297,8 @@
     logits_of(2, 3)
     logits_of(1, 4)
 
-    lane = lax.broadcasted_iota(I32, (128, 128), 1)
-
     def hit_of(i, j):
-        wide = jnp.broadcast_to(tgt[i:i + 1, :].astype(F32), (128, 128)).T.astype(I32)
-        return wide - col * CODES == lane + j * 128
+        return tw[i * 128:(i + 1) * 128, :] == lane + j * 128
 
     for i in range(4):
         rows = slice(i * 128, (i + 1) * 128)
@@ -325,11 +327,20 @@
             dl[i * 128:(i + 1) * 128, j * 128:(j + 1) * 128] = d.astype(BF16)
             dlt[j * 128:(j + 1) * 128, i * 128:(i + 1) * 128] = d.T.astype(BF16)
 
+    def sib_block(dz):
+        v = dot(dl[...], wf[((z + dz) % NZ) * 2 + 1 - k], NT).astype(BF16)
+        for h in range(2):
+            gqs[dz, h] = v[:, h * 128:(h + 1) * 128]
+        send(("gs", dz), gqs.at[dz], sibr.at[dz], sib)
+
+    def own_block(dz):
+        v = dot(dl[...], wf[((z + dz) % NZ) * 2 + k], NT).astype(BF16)
+        for h in range(2):
+            gqo[dz, h] = v[:, h * 128:(h + 1) * 128]
+
     def grad_block(dz):
-        at = ((z + dz) % NZ) * 2
-        gqs[dz] = dot(dl[...], wf[at + 1 - k], NT).astype(BF16)
-        send(("gs", dz), gqs.at[dz], sibr.at[dz], sib)
-        gqo[dz] = dot(dl[...], wf[at + k], NT).astype(BF16)
+        sib_block(dz)
+        own_block(dz)
 
     def pair_up(dz):
         recv(("gs", dz), sibr.at[dz])
@@ -337,10 +348,10 @@
 
     def sub_block(dx, dy):
         s = slot(dx, dy)
-        gt[s] = dot(dlt[...], qf[s]).astype(BF16)
+        gt[s] = dot(dlt[...], jnp.concatenate([qf[s, 0], qf[s, 1]], axis=1)).astype(BF16)
 
     def zpart(dz, h):
-        return gqo.at[dz % NZ, pl.ds(h * HALF, HALF), :]
+        return gqo.at[dz % NZ, h]
 
     def zsend(way, d, h):
         send(("z", way, d, h), zpart(way * (d + 1), h), zr.at[(1 - way) // 2, d, h], zn(way))
@@ -385,15 +396,18 @@
             part[...].astype(F32) + xl[half, j, 0].astype(F32) + xl[half, j, 1].astype(F32)
         ).astype(BF16)
 
-    grad_block(4)
-    grad_block(3)
-    grad_block(5)
+    sib_block(4)
     sub_block(2, 2)
+    for half in range(2):
+        x_start(half, 2)
+    own_block(4)
+    sib_block(3)
+    sib_block(5)
     pair_up(4)
     zsend(1, 3, 0)
     zsend(-1, 3, 1)
-    for half in range(2):
-        x_start(half, 2)
+    own_block(3)
+    own_block(5)
     pair_up(3)
     pair_up(5)
     zsend(1, 2, 1)
@@ -455,39 +469,51 @@
     for half in range(2):
         x_end(half, 0)
 
-    for way in (1, -1):
-        for h in range(2):
+    for h in range(2):
+        for way in (1, -1):
             recv(("z", way, 0, h), zr.at[(1 - way) // 2, 0, h])
-    for h in range(2):
-        rows = pl.ds(h * HALF, HALF)
-        total = gqo[0, rows, :].astype(F32) + zr[0, 0, h].astype(F32) + zr[1, 0, h].astype(F32)
-        gh_o[rows, :] = total.astype(BF16)
-    for t in range(8):
-        moved = dot(mm[t * 128:(t + 1) * 128, :], gh_o[...]).astype(BF16)
-        outb[2 * t] = moved[:CAP]
-        outb[2 * t + 1] = moved[CAP:]
-    for rel in range(1, NR):
-        to = (row + rel) % NR
-        send(("ret", rel), outb.at[to], ret_o.at[row], rdev(to))
-    ret_o[row] = outb[row]
+        total = gqo[0, h].astype(F32) + zr[0, 0, h].astype(F32) + zr[1, 0, h].astype(F32)
+        ghb[h] = total.astype(BF16)
+        gh_o[:, h * 128:(h + 1) * 128] = ghb[h]
+        for t in range(4):
+            moved = dot(mm[t * 256:(t + 1) * 256, :], ghb[h]).astype(BF16)
+            for u in range(4):
+                outb[h, 4 * t + u] = moved[u * CAP:(u + 1) * CAP]
+        for rel in range(1, NR):
+            to = (row + rel) % NR
+            send((f"ret{h}", rel), outb.at[h, to], ret_o.at[h, row], rdev(to))
+        ret_o[h, row] = outb[h, row]
+    for t in range(NR // 2):
+        ask_o[t:t + 1, :] = jnp.concatenate(
+            [askv[2 * t, 0:1, :CAP], askv[2 * t + 1, 0:1, :CAP]], axis=1
+        )
     for half in range(2):
         x_end(half, 4)
     gs_o[...] = gt[row].astype(F32).T.astype(BF16)
-    for rel in range(1, NR):
-        recv(("ret", rel), ret_o.at[(row - rel + NR) % NR])
+    for h in range(2):
+        for rel in range(1, NR):
+            recv((f"ret{h}", rel), ret_o.at[h, (row - rel + NR) % NR])
 
     for c in sent:
         c.wait_send()
 
-    @pl.loop(1, NR)
-    def _(rel):
-        cp(IDS(("serve", 0)) + rel, srv.at[0], fet.at[0], sib).wait_send()
-
-
-def scatter_kernel(ret, ask, out):
-    base = pl.program_id(0) * 256
-    hits = (ask[...] - base == lax.broadcasted_iota(I32, (256, NR * CAP), 0)).astype(F32).astype(BF16)
-    out[...] = dot(hits, ret[...]).astype(BF16)
+    for h in range(2):
+        @pl.loop(1, NR)
+        def _(rel, h=h):
+            cp(IDS((f"serve{h}", 0)) + rel, srv.at[h, 0], fet.at[h, 0], sib).wait_send()
+
+
+def scatter_kernel(ret, ask, gh, gs, loss, codes_o, gh_o, gs_o, loss_o):
+    base = pl.program_id(0) * TILE
+    rows = jnp.concatenate([ret[h].reshape(NR * CAP, 128) for h in range(2)], axis=1)
+    slots = lax.broadcasted_iota(I32, (TILE, 128), 0)
+    hits = jnp.concatenate(
+        [(ask[t:t + 1, :] - base == slots).astype(F32).astype(BF16) for t in range(8)], axis=1
+    )
+    codes_o[...] = dot(hits, rows).astype(BF16)
+    gh_o[...] = gh[...]
+    gs_o[...] = gs[...]
+    loss_o[...] = loss[...]
 
 
 def per_device(hidden_rows, code_table, labels, targets, sub_codebook):
@@ -498,38 +524,42 @@
             jax.ShapeDtypeStruct((4, 128), F32),
             jax.ShapeDtypeStruct((ROWS, FEAT), BF16),
             jax.ShapeDtypeStruct((FEAT, CODES), BF16),
-            jax.ShapeDtypeStruct((NR, CAP, FEAT), BF16),
-            jax.ShapeDtypeStruct((NR, 128), I32),
+            jax.ShapeDtypeStruct((2, NR, CAP, 128), BF16),
+            jax.ShapeDtypeStruct((8, 128), I32),
         ),
         in_specs=[vmem, pl.BlockSpec(memory_space=pl.ANY), vmem, vmem, vmem],
         out_specs=[vmem] * 5,
         scratch_shapes=[
             pltpu.VMEM((NR, FEAT, CODES), BF16),
-            pltpu.VMEM((NC, ROWS, FEAT), BF16),
-            pltpu.VMEM((2, CHUNK, FEAT), BF16),
-            pltpu.VMEM((TABLE, FEAT), F32),
+            pltpu.VMEM((NC, 2, ROWS, 128), BF16),
+            pltpu.VMEM((TABLE // CHUNK, CHUNK, FEAT), BF16),
+            pltpu.VMEM((2, TABLE, 128), F32),
             pltpu.VMEM((NR, 8, 128), I32),
             pltpu.VMEM((NR, 8, 128), I32),
+            pltpu.VMEM((NR, 128), I32),
             pltpu.SMEM((NR, 128), I32),
-            pltpu.VMEM((CAP, FEAT), F32),
-            pltpu.VMEM((NR, CAP, FEAT), BF16),
-            pltpu.VMEM((NR, CAP, FEAT), BF16),
+            pltpu.VMEM((CAP, 128), F32),
+            pltpu.VMEM((2, NR, CAP, 128), BF16),
+            pltpu.VMEM((2, NR, CAP, 128), BF16),
             pltpu.VMEM((ROWS, NR * CAP), BF16),
             pltpu.VMEM((NR * CAP, ROWS), BF16),
+            pltpu.VMEM((ROWS, 128), I32),
             pltpu.VMEM((ROWS, CODES), F32),
             pltpu.VMEM((ROWS, CODES), BF16),
             pltpu.VMEM((CODES, ROWS), BF16),
             pltpu.VMEM((8, 128), F32),
             pltpu.VMEM((NC, 8, 128), F32),
-            pltpu.VMEM((NZ, ROWS, FEAT), BF16),
-            pltpu.VMEM((NZ, ROWS, FEAT), BF16),
-            pltpu.VMEM((NZ, ROWS, FEAT), BF16),
-            pltpu.VMEM((2, 4, 2, HALF, FEAT), BF16),
+            pltpu.VMEM((NZ, 2, ROWS, 128), BF16),
+            pltpu.VMEM((NZ, 2, ROWS, 128), BF16),
+            pltpu.VMEM((NZ, 2, ROWS, 128), BF16),
+            pltpu.VMEM((2, 4, 2, ROWS, 128), BF16),
             pltpu.VMEM((NR, CODES, FEAT), BF16),
             pltpu.VMEM((2, 5, 2, 128, FEAT), BF16),
             pltpu.VMEM((2, 5, 2, 256, FEAT), BF16),
-            pltpu.VMEM((NR, CAP, FEAT), BF16),
-            pltpu.SemaphoreType.DMA((4,)),
+            pltpu.VMEM((2, ROWS, 128), BF16),
+            pltpu.VMEM((2, NR, CAP, 128), BF16),
+            pltpu.SemaphoreType.DMA((2,)),
+            pltpu.SemaphoreType.DMA((TABLE // CHUNK,)),
             pltpu.SemaphoreType.DMA((N_IDS,)),
             pltpu.SemaphoreType.DMA((N_IDS,)),
         ],
@@ -538,17 +568,32 @@
         ),
         name="exchange_and_gradients",
     )(hidden_rows, code_table, labels.reshape(4, 128), targets.reshape(4, 128), sub_codebook)
-    grad_codes = pl.pallas_call(
+    steps = TABLE // TILE
+    grad_codes, grad_hidden, grad_sub, loss = pl.pallas_call(
         scatter_kernel,
-        grid=(TABLE // 256,),
+        grid=(steps,),
         in_specs=[
-            pl.BlockSpec((NR * CAP, FEAT), lambda i: (0, 0)),
-            pl.BlockSpec((1, NR * CAP), lambda i: (0, 0)),
+            pl.BlockSpec((2, NR, CAP, 128), lambda i: (0, 0, 0, 0)),
+            pl.BlockSpec((8, 128), lambda i: (0, 0)),
+            pl.BlockSpec((ROWS // steps, FEAT), lambda i: (i, 0)),
+            pl.BlockSpec((FEAT // steps, CODES), lambda i: (i, 0)),
+            pl.BlockSpec((4, 128), lambda i: (0, 0)),
         ],
-        out_specs=pl.BlockSpec((256, FEAT), lambda i: (i, 0)),
-        out_shape=jax.ShapeDtypeStruct((TABLE, FEAT), BF16),
+        out_specs=[
+            pl.BlockSpec((TILE, FEAT), lambda i: (i, 0)),
+            pl.BlockSpec((ROWS // steps, FEAT), lambda i: (i, 0)),
+            pl.BlockSpec((FEAT // steps, CODES), lambda i: (i, 0)),
+            pl.BlockSpec((4, 128), lambda i: (0, 0)),
+        ],
+        out_shape=[
+            jax.ShapeDtypeStruct((TABLE, FEAT), BF16),
+            jax.ShapeDtypeStruct((ROWS, FEAT), BF16),
+            jax.ShapeDtypeStruct((FEAT, CODES), BF16),
+            jax.ShapeDtypeStruct((4, 128), F32),
+        ],
+        compiler_params=pltpu.CompilerParams(vmem_limit_bytes=50 * 1024 * 1024),
         name="grad_codes",
-    )(returned.reshape(NR * CAP, FEAT), asked[:, :CAP].reshape(1, NR * CAP))
+    )(returned, asked, grad_hidden, grad_sub, loss)
     return loss.reshape(ROWS), grad_hidden, grad_codes, grad_sub
 
 

time: 120 us -> 110 us (0.917)
  Pallas kernels: 116 us -> 105 us
    pallas_call x1, Pallas kernels: 17 us -> 6.04 us  [per_device(): pl.pallas_call(scatter_kernel, grid=(steps,), in_specs=[pl.BlockSpec((2,...]
    unnamed x9 -> x10, local copies, waits for them, and re-layouts: 2 us -> 4.28 us
    reshape x1 -> x0, local copies, waits for them, and re-layouts: 1.42 us -> none  [per_device(): asked[:, :CAP].reshape(1, NR * CAP)]
where the time goes in v2:
time: 110 us
  Pallas kernels  105 us (95%)
  local copies, waits for them, and re-layouts  4.28 us (4%)
    pallas_call x1, Pallas kernels, per_device(): pl.pallas_call(main_kernel, out_shape=(jax.ShapeDtypeStruct((4, 128), F32...  98.6 us
    pallas_call x1, Pallas kernels, per_device(): pl.pallas_call(scatter_kernel, grid=(steps,), in_specs=[pl.BlockSpec((2,...  6.04 us
    unnamed x10, local copies, waits for them, and re-layouts  4.28 us

profile of v2, /device:TPU:24, one launch (start us, length us, event | category | flops | bytes accessed | tf_op | source)
XLA Modules:
  0.0 109.6 jit_solution(4028123383442147681)
XLA Ops:
  0.6 98.6 %exchange_and_gradients.1 = (f32[4,128]{1,0:T(4,128)}, bf16[512,256]{1,0:T(8,128)(2,1)}, bf16[256,512]{1,0:T(8,128)(2,1)}, bf16[2,16,64,128]{3,2,1,0:T(8,128)(2,1)}, s32[8,128]{1,0:T(8,128)}) custom-call(bf16[512,256]{1,0:T(8,128)(2,1)} %hid.1, bf16[8192,256]{1,0:T(8,128)(2,1)} %table.1, s32[4,128]{1,0:T(4,128)} %bitcast.3, s32[4,128]{1,0:T(4,128)} %bitcast.4, ...), custom_call_target="tpu_custom_call" | custom-call | tf_op jit(solution)/shard_map/exchange_and_gradients/pallas_call | solution.py:521
  99.2 0.0 copy-start
  99.2 1.0 copy-done
  100.3 0.0 copy-start.1
  100.3 0.9 copy-done.1
  101.2 0.0 copy-start.2
  101.2 0.9 copy-done.2
  102.2 0.0 copy-start.3
  102.2 0.7 copy-done.3
  102.9 0.0 copy-start.4
  102.9 0.7 copy-done.4
  103.5 6.0 %grad_codes.1 = (bf16[8192,256]{1,0:T(8,128)(2,1)}, bf16[512,256]{1,0:T(8,128)(2,1)}, bf16[256,512]{1,0:T(8,128)(2,1)}, f32[4,128]{1,0:T(4,128)}) custom-call(bf16[2,16,64,128]{3,2,1,0:T(8,128)(2,1)S(1)} %copy-done, s32[8,128]{1,0:T(8,128)S(1)} %copy-done.3, bf16[512,256]{1,0:T(8,128)(2,1)S(1)} %copy-done.1, bf16[256,512]{1,0:T(8,128)(2,1)S(1)} %copy-done.2, ...), custom_call_target="tpu_custom_call" | custom-call | tf_op jit(solution)/shard_map/grad_codes/pallas_call | solution.py:572
Async XLA Ops:
  99.2 1.0 copy-start
  100.3 0.9 copy-start.1
  101.2 0.9 copy-start.2
  102.2 0.7 copy-start.3
  102.9 0.7 copy-start.4

commit v3 on v2

--- a/solution.py
+++ b/solution.py
@@ -200,23 +200,34 @@
     to_smem.start()
     to_smem.wait()
 
-    def gather(h, r):
+    def gather(r):
         @pl.loop(0, CAP // 16)
         def _(t):
+            picks = [asks[r, t * 16 + u] & (TABLE - 1) for u in range(16)]
+            rows = [(tf[0, pl.ds(i, 1), :], tf[1, pl.ds(i, 1), :]) for i in picks]
             for u in range(16):
-                i = asks[r, t * 16 + u] & (TABLE - 1)
-                srv32[pl.ds(t * 16 + u, 1), :] = tf[h, pl.ds(i, 1), :]
-
-    for h in range(2):
-        @pl.loop(1, NR)
-        def _(rel, h=h):
-            to = (row + rel) % NR
-            gather(h, to)
-            srv[h, to] = srv32[...].astype(BF16)
-            cp(IDS((f"serve{h}", 0)) + rel, srv.at[h, to], fet.at[h, row], rdev(to)).start()
-
-        gather(h, row)
-        fet[h, row] = srv32[...].astype(BF16)
+                for h in range(2):
+                    srv32[h, pl.ds(t * 16 + u, 1), :] = rows[u][h]
+
+    def serve(h, rel):
+        to = (row + rel) % NR
+        cp(IDS((f"serve{h}", 0)) + rel, srv.at[h, to], fet.at[h, row], rdev(to)).start()
+
+    @pl.loop(1, NR)
+    def _(rel):
+        to = (row + rel) % NR
+        gather(to)
+        for h in range(2):
+            srv[h, to] = srv32[h].astype(BF16)
+        serve(0, rel)
+
+    @pl.loop(1, NR)
+    def _(rel):
+        serve(1, rel)
+
+    gather(row)
+    for h in range(2):
+        fet[h, row] = srv32[h].astype(BF16)
 
     for half in range(2):
         for side in range(2):
@@ -234,21 +245,20 @@
             recv((f"serve{h}", rel), fet.at[h, (row - rel + NR) % NR])
         code = dot(pm[...], fet[h].reshape(NR * CAP, 128))
         qf[col, h] = (hid[:, h * 128:(h + 1) * 128].astype(F32) + code).astype(BF16)
+        send(("qs", 0, h), qpart(col, h), qpart(col, h), sib)
         for way in (1, -1):
             send(("q", way, 1, h), qpart(col, h), qpart(col, h), zn(way))
-        send(("qs", 0, h), qpart(col, h), qpart(col, h), sib)
-
-    def q_step(s):
-        for h in range(2):
-            for way in (1, -1):
-                if s == 4 and (way == 1) != (h == 0):
-                    continue
-                at = ((z - way * s + NZ) % NZ) * 2 + k
-                piece = qpart(at, h)
-                recv(("q", way, s, h), piece)
-                if s < 3 or (s == 3 and (way == 1) == (h == 0)):
-                    send(("q", way, s + 1, h), piece, piece, zn(way))
-                send(("qs", (-way * s) % NZ, h), piece, piece, sib)
+
+    def q_step(s, h):
+        for way in (1, -1):
+            if s == 4 and (way == 1) != (h == 0):
+                continue
+            at = ((z - way * s + NZ) % NZ) * 2 + k
+            piece = qpart(at, h)
+            recv(("q", way, s, h), piece)
+            send(("qs", (-way * s) % NZ, h), piece, piece, sib)
+            if s < 3 or (s == 3 and (way == 1) == (h == 0)):
+                send(("q", way, s + 1, h), piece, piece, zn(way))
 
     def logits_of(n_ways, s):
         for dz in ([s, NZ - s] if 0 < s < 4 else [s]):
@@ -268,6 +278,10 @@
     for half in range(2):
         w_last(half, 4)
         w_own(half, 2)
+    for j in (3, 1):
+        for half in range(2):
+            for side in range(2):
+                w_mid(half, j, side)
     for i in range(4):
         tw[i * 128:(i + 1) * 128, :] = (
             jnp.broadcast_to(tgt[i:i + 1, :].astype(F32), (128, 128)).T.astype(I32) - col * CODES
@@ -276,24 +290,24 @@
         mm[t * 128:(t + 1) * 128, :] = (
             place == lax.broadcasted_iota(I32, (128, ROWS), 0) + t * 128
         ).astype(F32).astype(BF16)
-    q_step(1)
-    for j in (3, 1):
-        for half in range(2):
-            for side in range(2):
-                w_mid(half, j, side)
-    q_step(2)
+    lg[...] = jnp.zeros((ROWS, CODES), F32)
+    for h in range(2):
+        q_step(1, h)
     for half in range(2):
         for side in range(2):
             w_mid(half, 2, side)
+    for h in range(2):
+        q_step(2, h)
     for j in (0, 3, 1, 2):
         for half in range(2):
             w_last(half, j)
-    lg[...] = jnp.zeros((ROWS, CODES), F32)
     logits_of(1, 0)
-    q_step(3)
+    q_step(3, 0)
     logits_of(2, 1)
+    q_step(3, 1)
     logits_of(2, 2)
-    q_step(4)
+    for h in range(2):
+        q_step(4, h)
     logits_of(2, 3)
     logits_of(1, 4)
 
@@ -538,7 +552,7 @@
             pltpu.VMEM((NR, 8, 128), I32),
             pltpu.VMEM((NR, 128), I32),
             pltpu.SMEM((NR, 128), I32),
-            pltpu.VMEM((CAP, 128), F32),
+            pltpu.VMEM((2, CAP, 128), F32),
             pltpu.VMEM((2, NR, CAP, 128), BF16),
             pltpu.VMEM((2, NR, CAP, 128), BF16),
             pltpu.VMEM((ROWS, NR * CAP), BF16),
@@ -591,7 +605,7 @@
             jax.ShapeDtypeStruct((FEAT, CODES), BF16),
             jax.ShapeDtypeStruct((4, 128), F32),
         ],
-        compiler_params=pltpu.CompilerParams(vmem_limit_bytes=50 * 1024 * 1024),
+        compiler_params=pltpu.CompilerParams(vmem_limit_bytes=60 * 1024 * 1024),
         name="grad_codes",
     )(returned, asked, grad_hidden, grad_sub, loss)
     return loss.reshape(ROWS), grad_hidden, grad_codes, grad_sub

time: 110 us -> 107 us (0.973)
  local copies, waits for them, and re-layouts: 4.28 us -> 0 us
    unnamed x10 -> x0, local copies, waits for them, and re-layouts: 4.28 us -> none
    pallas_call x1, Pallas kernels: 6.04 us -> 7.25 us  [per_device(): pl.pallas_call(scatter_kernel, grid=(steps,), in_specs=[pl.BlockSpec((2,...]
where the time goes in v3:
time: 107 us
  Pallas kernels  106 us (99%)
    pallas_call x1, Pallas kernels, per_device(): pl.pallas_call(main_kernel, out_shape=(jax.ShapeDtypeStruct((4, 128), F32...  99.1 us
    pallas_call x1, Pallas kernels, per_device(): pl.pallas_call(scatter_kernel, grid=(steps,), in_specs=[pl.BlockSpec((2,...  7.25 us

profile of v3, /device:TPU:24, one launch (start us, length us, event | category | flops | bytes accessed | tf_op | source)
XLA Modules:
  0.0 107.0 jit_solution(4290414502983043719)
XLA Ops:
  0.6 99.1 %exchange_and_gradients.1 = (f32[4,128]{1,0:T(4,128)}, bf16[512,256]{1,0:T(8,128)(2,1)}, bf16[256,512]{1,0:T(8,128)(2,1)}, bf16[2,16,64,128]{3,2,1,0:T(8,128)(2,1)}, s32[8,128]{1,0:T(8,128)}) custom-call(bf16[512,256]{1,0:T(8,128)(2,1)} %hid.1, bf16[8192,256]{1,0:T(8,128)(2,1)} %table.1, s32[4,128]{1,0:T(4,128)} %bitcast.3, s32[4,128]{1,0:T(4,128)} %bitcast.4, ...), custom_call_target="tpu_custom_call" | custom-call | tf_op jit(solution)/shard_map/exchange_and_gradients/pallas_call | solution.py:535
  99.8 7.3 %grad_codes.1 = (bf16[8192,256]{1,0:T(8,128)(2,1)}, bf16[512,256]{1,0:T(8,128)(2,1)}, bf16[256,512]{1,0:T(8,128)(2,1)}, f32[4,128]{1,0:T(4,128)}) custom-call(bf16[2,16,64,128]{3,2,1,0:T(8,128)(2,1)} %get-tuple-element.13.ret, s32[8,128]{1,0:T(8,128)} %get-tuple-element.14.ask, bf16[512,256]{1,0:T(8,128)(2,1)} %get-tuple-element.15.gh, ...), custom_call_target="tpu_custom_call" | custom-call | tf_op jit(solution)/shard_map/grad_codes/pallas_call | solution.py:586

commit v4 on v3

--- a/solution.py
+++ b/solution.py
@@ -100,6 +100,28 @@
     def recv(name, dst):
         cp(IDS(name), dst, dst, sib).wait_recv()
 
+    def each_send(name, count, copy):
+        @pl.loop(1, count)
+        def _(rel):
+            src, dst, dev = copy(rel)
+            cp(IDS((name, 0)) + rel, src, dst, dev).start()
+
+    def each_recv(name, count, dst):
+        @pl.loop(1, count)
+        def _(rel):
+            cp(IDS((name, 0)) + rel, dst(rel), dst(rel), sib).wait_recv()
+
+    def each_sent(name, count, src):
+        @pl.loop(1, count)
+        def _(rel):
+            cp(IDS((name, 0)) + rel, src, src, sib).wait_send()
+
+    def row_at(rel):
+        return (row + rel + NR) % NR
+
+    def col_at(rel):
+        return (col + rel + NC) % NC
+
     own_w = pltpu.make_async_copy(wsub, wf.at[row], lsem.at[0])
     own_w.start()
 
@@ -112,9 +134,11 @@
         table_copy(i).start()
 
     barrier = pltpu.get_barrier_semaphore()
-    for rel in range(1, 16):
-        pl.semaphore_signal(barrier, inc=1, device_id=rdev((row + rel) % NR), device_id_type=MESH)
-        pl.semaphore_signal(barrier, inc=1, device_id=cdev((col + rel) % NC), device_id_type=MESH)
+
+    @pl.loop(1, 16)
+    def _(rel):
+        pl.semaphore_signal(barrier, inc=1, device_id=rdev(row_at(rel)), device_id_type=MESH)
+        pl.semaphore_signal(barrier, inc=1, device_id=cdev(col_at(rel)), device_id_type=MESH)
 
     lab_row = jnp.concatenate([lab[i:i + 1, :] for i in range(4)], axis=1)
     owner = lax.shift_right_logical(lab_row, 13)
@@ -136,9 +160,7 @@
     place = owner * CAP + rank
 
     pl.semaphore_wait(barrier, 30)
-    for rel in range(1, NR):
-        to = (row + rel) % NR
-        send(("want", rel), wbuf.at[to], askv.at[row], rdev(to))
+    each_send("want", NR, lambda rel: (wbuf.at[row_at(rel)], askv.at[row], rdev(row_at(rel))))
     own_w.wait()
 
     def whalf(s, half, a=0, n=128):
@@ -181,6 +203,51 @@
             v = tb[i, pl.ds(t * 128, 128), :].astype(F32)
             for h in range(2):
                 tf[h, pl.ds(i * CHUNK + t * 128, 128), :] = v[:, h * 128:(h + 1) * 128]
+
+    askv[row] = wbuf[row]
+    each_recv("want", NR, lambda rel: askv.at[row_at(-rel)])
+    for r in range(NR):
+        askr[r:r + 1, :] = askv[r, 0:1, :]
+    to_smem = pltpu.make_async_copy(askr, asks, lsem.at[1])
+    to_smem.start()
+    to_smem.wait()
+
+    def gather(r):
+        @pl.loop(0, CAP // 16)
+        def _(t):
+            picks = [asks[r, t * 16 + u] & (TABLE - 1) for u in range(16)]
+            rows = [(tf[0, pl.ds(i, 1), :], tf[1, pl.ds(i, 1), :]) for i in picks]
+            for u in range(16):
+                for h in range(2):
+                    srv32[h, pl.ds(t * 16 + u, 1), :] = rows[u][h]
+
+    def serve(h, rel):
+        to = (row + rel) % NR
+        cp(IDS((f"serve{h}", 0)) + rel, srv.at[h, to], fet.at[h, row], rdev(to)).start()
+
+    @pl.loop(1, NR)
+    def _(rel):
+        to = (row + rel) % NR
+        gather(to)
+        for h in range(2):
+            srv[h, to] = srv32[h].astype(BF16)
+        serve(0, rel)
+
+    @pl.loop(1, NR)
+    def _(rel):
+        serve(1, rel)
+
+    gather(row)
+    for h in range(2):
+        fet[h, row] = srv32[h].astype(BF16)
+
+    for half in range(2):
+        for side in range(2):
+            w_mid(half, 4, side)
+            w_own(half, 3 - 2 * side)
+    for half in range(2):
+        for side in range(2):
+            w_mid(half, 0, side)
 
     place_f = place.astype(F32)
     lane = lax.broadcasted_iota(I32, (128, 128), 1)
@@ -191,58 +258,11 @@
                 wide == lane + t * 128
             ).astype(F32).astype(BF16)
 
-    askv[row] = wbuf[row]
-    for rel in range(1, NR):
-        recv(("want", rel), askv.at[(row - rel + NR) % NR])
-    for r in range(NR):
-        askr[r:r + 1, :] = askv[r, 0:1, :]
-    to_smem = pltpu.make_async_copy(askr, asks, lsem.at[1])
-    to_smem.start()
-    to_smem.wait()
-
-    def gather(r):
-        @pl.loop(0, CAP // 16)
-        def _(t):
-            picks = [asks[r, t * 16 + u] & (TABLE - 1) for u in range(16)]
-            rows = [(tf[0, pl.ds(i, 1), :], tf[1, pl.ds(i, 1), :]) for i in picks]
-            for u in range(16):
-                for h in range(2):
-                    srv32[h, pl.ds(t * 16 + u, 1), :] = rows[u][h]
-
-    def serve(h, rel):
-        to = (row + rel) % NR
-        cp(IDS((f"serve{h}", 0)) + rel, srv.at[h, to], fet.at[h, row], rdev(to)).start()
-
-    @pl.loop(1, NR)
-    def _(rel):
-        to = (row + rel) % NR
-        gather(to)
-        for h in range(2):
-            srv[h, to] = srv32[h].astype(BF16)
-        serve(0, rel)
-
-    @pl.loop(1, NR)
-    def _(rel):
-        serve(1, rel)
-
-    gather(row)
-    for h in range(2):
-        fet[h, row] = srv32[h].astype(BF16)
-
-    for half in range(2):
-        for side in range(2):
-            w_mid(half, 4, side)
-            w_own(half, 3 - 2 * side)
-    for half in range(2):
-        for side in range(2):
-            w_mid(half, 0, side)
-
     def qpart(s, h):
         return qf.at[s, h]
 
     for h in range(2):
-        for rel in range(1, NR):
-            recv((f"serve{h}", rel), fet.at[h, (row - rel + NR) % NR])
+        each_recv(f"serve{h}", NR, lambda rel: fet.at[h, row_at(-rel)])
         code = dot(pm[...], fet[h].reshape(NR * CAP, 128))
         qf[col, h] = (hid[:, h * 128:(h + 1) * 128].astype(F32) + code).astype(BF16)
         send(("qs", 0, h), qpart(col, h), qpart(col, h), sib)
@@ -325,10 +345,8 @@
         stat_s[i:i + 1, :] = pair[0:1, :]
         stat_s[4 + i:5 + i, :] = pair[1:2, :]
     stat_r[col] = stat_s[...]
-    for rel in range(1, NC):
-        send(("stat", rel), stat_s, stat_r.at[col], cdev((col + rel) % NC))
-    for rel in range(1, NC):
-        recv(("stat", rel), stat_r.at[(col - rel + NC) % NC])
+    each_send("stat", NC, lambda rel: (stat_s, stat_r.at[col], cdev(col_at(rel))))
+    each_recv("stat", NC, lambda rel: stat_r.at[col_at(-rel)])
     logs = stat_r[:, 0:4, :]
     top = jnp.max(logs, axis=0)
     log_total = top + jnp.log(jnp.sum(jnp.exp(logs - top[None]), axis=0))
@@ -493,9 +511,7 @@
             moved = dot(mm[t * 256:(t + 1) * 256, :], ghb[h]).astype(BF16)
             for u in range(4):
                 outb[h, 4 * t + u] = moved[u * CAP:(u + 1) * CAP]
-        for rel in range(1, NR):
-            to = (row + rel) % NR
-            send((f"ret{h}", rel), outb.at[h, to], ret_o.at[h, row], rdev(to))
+        each_send(f"ret{h}", NR, lambda rel: (outb.at[h, row_at(rel)], ret_o.at[h, row], rdev(row_at(rel))))
         ret_o[h, row] = outb[h, row]
     for t in range(NR // 2):
         ask_o[t:t + 1, :] = jnp.concatenate(
@@ -505,16 +521,16 @@
         x_end(half, 4)
     gs_o[...] = gt[row].astype(F32).T.astype(BF16)
     for h in range(2):
-        for rel in range(1, NR):
-            recv((f"ret{h}", rel), ret_o.at[h, (row - rel + NR) % NR])
+        each_recv(f"ret{h}", NR, lambda rel: ret_o.at[h, row_at(-rel)])
 
     for c in sent:
         c.wait_send()
 
-    for h in range(2):
-        @pl.loop(1, NR)
-        def _(rel, h=h):
-            cp(IDS((f"serve{h}", 0)) + rel, srv.at[h, 0], fet.at[h, 0], sib).wait_send()
+    each_sent("want", NR, wbuf.at[0])
+    each_sent("stat", NC, stat_s)
+    for h in range(2):
+        each_sent(f"serve{h}", NR, srv.at[h, 0])
+        each_sent(f"ret{h}", NR, outb.at[h, 0])
 
 
 def scatter_kernel(ret, ask, gh, gs, loss, codes_o, gh_o, gs_o, loss_o):

time: 107 us -> 107 us (level)
  no operation moved by 1% of the time
where the time goes in v4:
time: 107 us
  Pallas kernels  107 us (100%)
    pallas_call x1, Pallas kernels, per_device(): pl.pallas_call(main_kernel, out_shape=(jax.ShapeDtypeStruct((4, 128), F32...  99.4 us
    pallas_call x1, Pallas kernels, per_device(): pl.pallas_call(scatter_kernel, grid=(steps,), in_specs=[pl.BlockSpec((2,...  7.25 us

profile of v4, /device:TPU:24, one launch (start us, length us, event | category | flops | bytes accessed | tf_op | source)
XLA Modules:
  0.0 107.3 jit_solution(13016357920155621009)
XLA Ops:
  0.6 99.4 %exchange_and_gradients.1 = (f32[4,128]{1,0:T(4,128)}, bf16[512,256]{1,0:T(8,128)(2,1)}, bf16[256,512]{1,0:T(8,128)(2,1)}, bf16[2,16,64,128]{3,2,1,0:T(8,128)(2,1)}, s32[8,128]{1,0:T(8,128)}) custom-call(bf16[512,256]{1,0:T(8,128)(2,1)} %hid.1, bf16[8192,256]{1,0:T(8,128)(2,1)} %table.1, s32[4,128]{1,0:T(4,128)} %bitcast.3, s32[4,128]{1,0:T(4,128)} %bitcast.4, ...), custom_call_target="tpu_custom_call" | custom-call | tf_op jit(solution)/shard_map/exchange_and_gradients/pallas_call | solution.py:551
  100.1 7.2 %grad_codes.1 = (bf16[8192,256]{1,0:T(8,128)(2,1)}, bf16[512,256]{1,0:T(8,128)(2,1)}, bf16[256,512]{1,0:T(8,128)(2,1)}, f32[4,128]{1,0:T(4,128)}) custom-call(bf16[2,16,64,128]{3,2,1,0:T(8,128)(2,1)} %get-tuple-element.13.ret, s32[8,128]{1,0:T(8,128)} %get-tuple-element.14.ask, bf16[512,256]{1,0:T(8,128)(2,1)} %get-tuple-element.15.gh, ...), custom_call_target="tpu_custom_call" | custom-call | tf_op jit(solution)/shard_map/grad_codes/pallas_call | solution.py:602

commit v5 on v3

--- a/solution.py
+++ b/solution.py
@@ -53,11 +53,11 @@
 
 
 def main_kernel(
-    hid, table, lab, tgt, wsub,
-    loss_o, gh_o, gs_o, ret_o, ask_o,
+    hid_h, table, lab, tgt, wsub,
+    loss_o, gh_h, gs_h, ret_h, ask_o,
     wf, qf, tb, tf, wbuf, askv, askr, asks, srv32, srv, fet, pm, mm, tw, lg, dl, dlt,
     stat_s, stat_r, gqo, gqs, sibr, zr, gt, xq, xl, ghb, outb,
-    lsem, tsem, ssem, rsem,
+    hid, gh_o, gs_o, ret_o, lsem, tsem, ssem, rsem,
 ):
     row = lax.axis_index("row")
     col = lax.axis_index("col")
@@ -102,6 +102,10 @@
 
     own_w = pltpu.make_async_copy(wsub, wf.at[row], lsem.at[0])
     own_w.start()
+    hid_in = pltpu.make_async_copy(hid_h, hid, lsem.at[2])
+    hid_in.start()
+    gh_out = pltpu.make_async_copy(gh_o, gh_h, lsem.at[3])
+    gs_out = pltpu.make_async_copy(gs_o, gs_h, lsem.at[4])
 
     def table_copy(i):
         return pltpu.make_async_copy(
@@ -239,6 +243,8 @@
 
     def qpart(s, h):
         return qf.at[s, h]
+
+    hid_in.wait()
 
     for h in range(2):
         for rel in range(1, NR):
@@ -497,6 +503,7 @@
             to = (row + rel) % NR
             send((f"ret{h}", rel), outb.at[h, to], ret_o.at[h, row], rdev(to))
         ret_o[h, row] = outb[h, row]
+    gh_out.start()
     for t in range(NR // 2):
         ask_o[t:t + 1, :] = jnp.concatenate(
             [askv[2 * t, 0:1, :CAP], askv[2 * t + 1, 0:1, :CAP]], axis=1
@@ -504,9 +511,11 @@
     for half in range(2):
         x_end(half, 4)
     gs_o[...] = gt[row].astype(F32).T.astype(BF16)
+    gs_out.start()
     for h in range(2):
         for rel in range(1, NR):
             recv((f"ret{h}", rel), ret_o.at[h, (row - rel + NR) % NR])
+        pltpu.make_async_copy(ret_o.at[h], ret_h.at[h], lsem.at[5 + h]).start()
 
     for c in sent:
         c.wait_send()
@@ -515,6 +524,11 @@
         @pl.loop(1, NR)
         def _(rel, h=h):
             cp(IDS((f"serve{h}", 0)) + rel, srv.at[h, 0], fet.at[h, 0], sib).wait_send()
+
+    gh_out.wait()
+    gs_out.wait()
+    for h in range(2):
+        pltpu.make_async_copy(ret_o.at[h], ret_h.at[h], lsem.at[5 + h]).wait()
 
 
 def scatter_kernel(ret, ask, gh, gs, loss, codes_o, gh_o, gs_o, loss_o):
@@ -532,6 +546,7 @@
 
 def per_device(hidden_rows, code_table, labels, targets, sub_codebook):
     vmem = pl.BlockSpec(memory_space=pltpu.VMEM)
+    hbm = pl.BlockSpec(memory_space=pl.ANY)
     loss, grad_hidden, grad_sub, returned, asked = pl.pallas_call(
         main_kernel,
         out_shape=(
@@ -541,8 +556,8 @@
             jax.ShapeDtypeStruct((2, NR, CAP, 128), BF16),
             jax.ShapeDtypeStruct((8, 128), I32),
         ),
-        in_specs=[vmem, pl.BlockSpec(memory_space=pl.ANY), vmem, vmem, vmem],
-        out_specs=[vmem] * 5,
+        in_specs=[hbm, hbm, vmem, vmem, hbm],
+        out_specs=[vmem, hbm, hbm, hbm, vmem],
         scratch_shapes=[
             pltpu.VMEM((NR, FEAT, CODES), BF16),
             pltpu.VMEM((NC, 2, ROWS, 128), BF16),
@@ -572,7 +587,11 @@
             pltpu.VMEM((2, 5, 2, 256, FEAT), BF16),
             pltpu.VMEM((2, ROWS, 128), BF16),
             pltpu.VMEM((2, NR, CAP, 128), BF16),
-            pltpu.SemaphoreType.DMA((2,)),
+            pltpu.VMEM((ROWS, FEAT), BF16),
+            pltpu.VMEM((ROWS, FEAT), BF16),
+            pltpu.VMEM((FEAT, CODES), BF16),
+            pltpu.VMEM((2, NR, CAP, 128), BF16),
+            pltpu.SemaphoreType.DMA((7,)),
             pltpu.SemaphoreType.DMA((TABLE // CHUNK,)),
             pltpu.SemaphoreType.DMA((N_IDS,)),
             pltpu.SemaphoreType.DMA((N_IDS,)),

time: 107 us -> 107 us (level)
  no operation moved by 1% of the time
where the time goes in v5:
time: 107 us; the launch traced here: 106 us
  Pallas kernels  106 us (99%)
    pallas_call x1, Pallas kernels, per_device(): pl.pallas_call(main_kernel, out_shape=(jax.ShapeDtypeStruct((4, 128), F32...  98.5 us
    pallas_call x1, Pallas kernels, per_device(): pl.pallas_call(scatter_kernel, grid=(steps,), in_specs=[pl.BlockSpec((2,...  7.25 us

profile of v5, /device:TPU:24, one launch (start us, length us, event | category | flops | bytes accessed | tf_op | source)
XLA Modules:
  0.0 106.4 jit_solution(12038190504626265963)
XLA Ops:
  0.6 98.5 %exchange_and_gradients.1 = (f32[4,128]{1,0:T(4,128)}, bf16[512,256]{1,0:T(8,128)(2,1)}, bf16[256,512]{1,0:T(8,128)(2,1)}, bf16[2,16,64,128]{3,2,1,0:T(8,128)(2,1)}, s32[8,128]{1,0:T(8,128)}) custom-call(bf16[512,256]{1,0:T(8,128)(2,1)} %hid_h.1, bf16[8192,256]{1,0:T(8,128)(2,1)} %table.1, s32[4,128]{1,0:T(4,128)} %bitcast.3, s32[4,128]{1,0:T(4,128)} %bitcast.4, ...), custom_call_target="tpu_custom_call" | custom-call | tf_op jit(solution)/shard_map/exchange_and_gradients/pallas_call | solution.py:550
  99.1 7.3 %grad_codes.1 = (bf16[8192,256]{1,0:T(8,128)(2,1)}, bf16[512,256]{1,0:T(8,128)(2,1)}, bf16[256,512]{1,0:T(8,128)(2,1)}, f32[4,128]{1,0:T(4,128)}) custom-call(bf16[2,16,64,128]{3,2,1,0:T(8,128)(2,1)} %get-tuple-element.13.ret, s32[8,128]{1,0:T(8,128)} %get-tuple-element.14.ask, bf16[512,256]{1,0:T(8,128)(2,1)} %get-tuple-element.15.gh, ...), custom_call_target="tpu_custom_call" | custom-call | tf_op jit(solution)/shard_map/grad_codes/pallas_call | solution.py:605

commit v6 on v5

--- a/solution.py
+++ b/solution.py
@@ -271,15 +271,13 @@
             for h in range(2):
                 recv(("qs", dz, h), qpart(((z + dz) % NZ) * 2 + 1 - k, h))
 
-        @pl.loop(0, 2 * n_ways)
+        @pl.loop(0, n_ways)
         def _(t):
-            dz = jnp.where(t % n_ways == 0, s, NZ - s)
-            core = t // n_ways
-            at = ((z + dz) % NZ) * 2 + core
+            at = ((z + jnp.where(t == 0, s, NZ - s)) % NZ) * 2
             for h in range(2):
                 rows = pl.ds(h * HALF, HALF)
-                q = jnp.concatenate([qf[at, 0, rows, :], qf[at, 1, rows, :]], axis=1)
-                lg[rows, :] += dot(q, wf[at])
+                q = jnp.concatenate([qf[at + c, g, rows, :] for c in range(2) for g in range(2)], axis=1)
+                lg[rows, :] += dot(q, wf[pl.ds(at, 2)].reshape(2 * FEAT, CODES))
 
     for half in range(2):
         w_last(half, 4)
@@ -312,9 +310,9 @@
     logits_of(2, 1)
     q_step(3, 1)
     logits_of(2, 2)
+    logits_of(2, 3)
     for h in range(2):
         q_step(4, h)
-    logits_of(2, 3)
     logits_of(1, 4)
 
     def hit_of(i, j):

time: 107 us -> 105 us (0.981)
    pallas_call x1, Pallas kernels: 98.5 us -> 97.3 us  [per_device(): pl.pallas_call(main_kernel, out_shape=(jax.ShapeDtypeStruct((4, 128), F32...]
where the time goes in v6:
time: 105 us
  Pallas kernels  105 us (100%)
    pallas_call x1, Pallas kernels, per_device(): pl.pallas_call(main_kernel, out_shape=(jax.ShapeDtypeStruct((4, 128), F32...  97.3 us
    pallas_call x1, Pallas kernels, per_device(): pl.pallas_call(scatter_kernel, grid=(steps,), in_specs=[pl.BlockSpec((2,...  7.25 us

profile of v6, /device:TPU:24, one launch (start us, length us, event | category | flops | bytes accessed | tf_op | source)
XLA Modules:
  0.0 105.2 jit_solution(9710788048499910929)
XLA Ops:
  0.6 97.3 %exchange_and_gradients.1 = (f32[4,128]{1,0:T(4,128)}, bf16[512,256]{1,0:T(8,128)(2,1)}, bf16[256,512]{1,0:T(8,128)(2,1)}, bf16[2,16,64,128]{3,2,1,0:T(8,128)(2,1)}, s32[8,128]{1,0:T(8,128)}) custom-call(bf16[512,256]{1,0:T(8,128)(2,1)} %hid_h.1, bf16[8192,256]{1,0:T(8,128)(2,1)} %table.1, s32[4,128]{1,0:T(4,128)} %bitcast.3, s32[4,128]{1,0:T(4,128)} %bitcast.4, ...), custom_call_target="tpu_custom_call" | custom-call | tf_op jit(solution)/shard_map/exchange_and_gradients/pallas_call | solution.py:548
  98.0 7.3 %grad_codes.1 = (bf16[8192,256]{1,0:T(8,128)(2,1)}, bf16[512,256]{1,0:T(8,128)(2,1)}, bf16[256,512]{1,0:T(8,128)(2,1)}, f32[4,128]{1,0:T(4,128)}) custom-call(bf16[2,16,64,128]{3,2,1,0:T(8,128)(2,1)} %get-tuple-element.13.ret, s32[8,128]{1,0:T(8,128)} %get-tuple-element.14.ask, bf16[512,256]{1,0:T(8,128)(2,1)} %get-tuple-element.15.gh, ...), custom_call_target="tpu_custom_call" | custom-call | tf_op jit(solution)/shard_map/grad_codes/pallas_call | solution.py:603
